TPU v7x, 1024 devices: a whole 4x4x32 slice. The times are simulated.
1024 devices in a mesh: dp: 64 (over y_lo, z), expert: 16 (over x, y_hi, core).
Axes of the slice: x: 4, y: 4 (y_hi: 2, y_lo: 2; y = y_hi * 2 + y_lo), z: 32, core: 2. Of those that a mesh axis runs over, the one named last changes fastest.
Arguments:
- tokens: bfloat16 [131072, 2048], P(('dp', 'expert')), may hold values from -6 to 6
- cotangent: bfloat16 [131072, 2048], P(('dp', 'expert')), may hold values from -6 to 6
- expert_ids: int32 [131072, 2], P(('dp', 'expert')), may hold values from 0 to 15, all different within a row; in each aligned block of 128 rows (0 to 127, 128 to 255, ...) at most 18 rows name the same one
- gate_values: bfloat16 [131072, 2], P(('dp', 'expert')), may hold values from 0.099609375 to 1
- gate_weights: bfloat16 [16, 2048, 512], P('expert'), may hold values from -0.125 to 0.125
- up_weights: bfloat16 [16, 2048, 512], P('expert'), may hold values from -0.125 to 0.125
- down_weights: bfloat16 [16, 512, 2048], P('expert'), may hold values from -0.25 to 0.25
Outputs:
- token_grads: bfloat16 [131072, 2048], P(('dp', 'expert'))
- down_grads: float32 [16, 512, 2048], P('expert', 'dp')
Inputs may be any that keep to these rules, and one draw needn't show every extreme that they name: `expert_ids`: within the rows of one device, each expert is named by at most 18 slots, and by exactly 18 slots in the rows of some device.
All inputs are finite; a program needn't handle non-finite values.
Results may differ from a plain program's by a relative error of at most 0.0065.
Values may be sent and summed in bfloat16 or wider, within the bound.
A program may use at most 64 MiB of HBM per device.

v0:
```python
import jax
import jax.numpy as jnp
from jax import lax
from jax.sharding import PartitionSpec as P


def body(tokens, cotangent, expert_ids, gate_values, gate_weights, up_weights, down_weights):
    experts_here = lax.axis_size("expert")
    tok_count, model_width = tokens.shape
    choices_per = expert_ids.shape[1]
    capacity = tok_count * choices_per * 9 // (8 * experts_here)
    slot_total = tok_count * choices_per
    flat_ids = expert_ids.reshape(slot_total)
    columns = jnp.arange(experts_here, dtype=jnp.int32)
    one_hot = (flat_ids[:, None] == columns[None, :]).astype(jnp.int32)
    earlier = jnp.cumsum(one_hot, axis=0) - one_hot
    position = jnp.sum(one_hot * earlier, axis=1)
    target = flat_ids * capacity + position
    slot_ids = jnp.arange(slot_total, dtype=jnp.int32)
    source = jnp.full((experts_here * capacity,), slot_total, jnp.int32).at[target].set(slot_ids)
    source_token = source // choices_per
    sent_rows = jnp.take(tokens, source_token, axis=0, mode="fill", fill_value=0).reshape(
        experts_here, capacity, model_width
    )
    sent_grads = jnp.take(cotangent, source_token, axis=0, mode="fill", fill_value=0).reshape(
        experts_here, capacity, model_width
    )
    sent_gates = jnp.take(
        gate_values.reshape(slot_total), source, axis=0, mode="fill", fill_value=0
    ).reshape(experts_here, capacity)
    w_gate = gate_weights[0]
    w_up = up_weights[0]
    w_down = down_weights[0]
    arrived = lax.all_to_all(sent_rows, "expert", split_axis=0, concat_axis=0, tiled=True).reshape(
        -1, model_width
    )
    pre_gate = jnp.dot(arrived, w_gate, preferred_element_type=jnp.float32)
    pre_up = jnp.dot(arrived, w_up, preferred_element_type=jnp.float32)
    sigmoid_of = jax.nn.sigmoid(pre_gate)
    activated = pre_gate * sigmoid_of
    hidden = (activated * pre_up).astype(jnp.bfloat16)
    arrived_grads, arrived_gates = (
        lax.all_to_all(sent_grads, "expert", split_axis=0, concat_axis=0, tiled=True),
        lax.all_to_all(sent_gates, "expert", split_axis=0, concat_axis=0, tiled=True),
    )
    scaled = (
        arrived_gates.reshape(-1)[:, None].astype(jnp.float32)
        * arrived_grads.reshape(-1, model_width).astype(jnp.float32)
    ).astype(jnp.bfloat16)
    contract_cols = (((1,), (1,)), ((), ()))
    hidden_back = lax.dot_general(scaled, w_down, contract_cols, preferred_element_type=jnp.float32)
    gate_back = (hidden_back * pre_up * sigmoid_of * (1.0 + pre_gate * (1.0 - sigmoid_of))).astype(
        jnp.bfloat16
    )
    up_back = (hidden_back * activated).astype(jnp.bfloat16)
    row_grads = lax.dot_general(
        gate_back, w_gate, contract_cols, preferred_element_type=jnp.float32
    )
    row_grads = (
        row_grads
        + lax.dot_general(up_back, w_up, contract_cols, preferred_element_type=jnp.float32)
    ).astype(jnp.bfloat16)
    returned = lax.all_to_all(
        row_grads.reshape(experts_here, capacity, model_width),
        "expert",
        split_axis=0,
        concat_axis=0,
        tiled=True,
    )
    picked = jnp.take(returned.reshape(-1, model_width), target, axis=0).astype(jnp.float32)
    token_grads = jnp.sum(picked.reshape(tok_count, choices_per, model_width), axis=1).astype(
        jnp.bfloat16
    )
    down_part = lax.psum_scatter(
        lax.dot_general(
            hidden, scaled, (((0,), (0,)), ((), ())), preferred_element_type=jnp.float32
        ),
        "dp",
        scatter_dimension=0,
        tiled=True,
    )
    return (token_grads, down_part[None])


def solution(mesh):
    return jax.shard_map(
        body,
        mesh=mesh,
        in_specs=(
            P(("dp", "expert"), None),
            P(("dp", "expert"), None),
            P(("dp", "expert"), None),
            P(("dp", "expert"), None),
            P("expert", None, None),
            P("expert", None, None),
            P("expert", None, None),
        ),
        out_specs=(P(("dp", "expert"), None), P("expert", "dp", None)),
        check_vma=False,
    )
```

profile of v0, /device:TPU:12, one launch (start us, length us, event | category | flops | bytes accessed | tf_op | source)
XLA Modules:
  0.0 388.8 jit_solution(2239267903110022182)
XLA Ops:
  7.2 0.8 broadcast_multiply_fusion
  8.0 0.8 copy.26
  10.2 0.8 copy.32
  11.2 1.4 scatter_custom_fusion
  12.7 2.4 gather_fusion
  15.7 6.6 %all-to-all-start = ((bf16[16,1,18]{2,1,0:T(2,128)(2,1)}), bf16[16,1,18]{2,1,0:T(2,128)(2,1)S(1)}, u32[]{:S(2)}, u32[]{:S(2)}) async-start(bf16[16,1,18]{2,1,0:T(2,128)(2,1)} %select_n.66), calls=%async_computation | async-start | bytes 16384 | tf_op jit(solution)/shard_map/all_to_all | solution.py:44
  22.4 3.0 gather_fusion.2
  25.3 3.0 gather_fusion.3
  28.3 2.9 broadcast_select_fusion.2
  31.2 2.4 reshape.144
  33.5 7.2 %all-to-all-start.2 = ((bf16[16,18,2048]{2,1,0:T(8,128)(2,1)}), bf16[16,18,2048]{2,1,0:T(8,128)(2,1)}, u32[]{:S(2)}, u32[]{:S(2)}) async-start(bf16[16,18,2048]{2,1,0:T(8,128)(2,1)} %reshape.144), calls=%async_computation.2 | async-start | bytes 3145728 | tf_op jit(solution)/shard_map/all_to_all | solution.py:34
  40.8 1.3 reshape.143
  42.1 20.1 %all-to-all-done.2 = bf16[16,18,2048]{2,1,0:T(8,128)(2,1)} async-done(((bf16[16,18,2048]{2,1,0:T(8,128)(2,1)}), bf16[16,18,2048]{2,1,0:T(8,128)(2,1)}, u32[]{:S(2)}, u32[]{:S(2)}) %all-to-all-start.2) | async-done | bytes 1179680 | tf_op jit(solution)/shard_map/all_to_all | solution.py:34
  62.2 6.5 %all-to-all-start.1 = ((bf16[16,18,2048]{2,1,0:T(8,128)(2,1)}), bf16[16,18,2048]{2,1,0:T(8,128)(2,1)}, u32[]{:S(2)}, u32[]{:S(2)}) async-start(bf16[16,18,2048]{2,1,0:T(8,128)(2,1)} %reshape.143), calls=%async_computation.1 | async-start | bytes 3145728 | tf_op jit(solution)/shard_map/all_to_all | solution.py:43
  68.9 2.4 reshape.145
  71.3 2.2 fusion.3
  74.3 15.9 %all-to-all-done.1 = bf16[16,18,2048]{2,1,0:T(8,128)(2,1)} async-done(((bf16[16,18,2048]{2,1,0:T(8,128)(2,1)}), bf16[16,18,2048]{2,1,0:T(8,128)(2,1)}, u32[]{:S(2)}, u32[]{:S(2)}) %all-to-all-start.1) | async-done | bytes 1179680 | tf_op jit(solution)/shard_map/all_to_all | solution.py:43
  90.3 2.7 reshape.150
  93.0 5.0 %fusion.10 = f32[512,2048]{1,0:T(8,128)} fusion(f32[288,2048]{1,0:T(8,128)} %reshape.150, f32[288]{0:T(512)S(1)} %reshape.149, f32[288,512]{1,0:T(8,128)S(1)} %fusion.6, f32[288,512]{1,0:T(8,128)S(1)} %fusion.3), kind=kOutput, calls=%fused_computation.19 | convolution fusion | flops 606044160 | bytes 7734400 | tf_op jit(solution)/shard_map/dot_general | solution.py:75
  98.0 2.9 multiply_convert_fusion
  100.9 2.4 convert_element_type.62
  103.3 2.8 fusion.8
  106.1 0.9 fusion.1
  107.6 1.9 fusion
  109.6 1.4 reshape.146
  111.0 6.7 %all-to-all-start.3 = ((bf16[16,18,2048]{2,1,0:T(8,128)(2,1)}), bf16[16,18,2048]{2,1,0:T(8,128)(2,1)}, u32[]{:S(2)}, u32[]{:S(2)}) async-start(bf16[16,18,2048]{2,1,0:T(8,128)(2,1)} %reshape.146), calls=%async_computation.3 | async-start | bytes 3145728 | tf_op jit(solution)/shard_map/all_to_all | solution.py:63
  118.0 21.1 %all-to-all-done.3 = bf16[16,18,2048]{2,1,0:T(8,128)(2,1)} async-done(((bf16[16,18,2048]{2,1,0:T(8,128)(2,1)}), bf16[16,18,2048]{2,1,0:T(8,128)(2,1)}, u32[]{:S(2)}, u32[]{:S(2)}) %all-to-all-start.3) | async-done | bytes 1179680 | tf_op jit(solution)/shard_map/all_to_all | solution.py:63
  139.1 1.6 reshape.147
  140.7 2.3 gather_fusion.1
  143.0 1.7 gather.15
  144.8 3.2 fusion.12
  148.0 234.0 %reduce-scatter.2.cloned.1.call-done = f32[8,2048]{1,0:T(8,128)} async-done(((f32[512,2048]{1,0:T(8,128)}), f32[8,2048]{1,0:T(8,128)}) %reduce-scatter.2.cloned.1.call-update) | async-done | bytes 65552 | tf_op jit(solution)/shard_map/reduce_scatter | solution.py:74
  (47 shorter events, 4.4 us)
Async XLA Ops:
  7.2 64.1 %copy-start = (bf16[1,2048,512]{2,1,0:T(8,128)(2,1)S(1)}, bf16[1,2048,512]{2,1,0:T(8,128)(2,1)}, u32[]{:S(2)}) copy-start(bf16[1,2048,512]{2,1,0:T(8,128)(2,1)} %param.13) | copy-start | bytes 6291460
  7.2 15.2 %copy-start.1 = (bf16[128,2048]{1,0:T(8,128)(2,1)S(1)}, bf16[128,2048]{1,0:T(8,128)(2,1)}, u32[]{:S(2)}) copy-start(bf16[128,2048]{1,0:T(8,128)(2,1)} %param.10) | copy-start | bytes 1572868
  15.7 17.8 %all-to-all-start = ((bf16[16,1,18]{2,1,0:T(2,128)(2,1)}), bf16[16,1,18]{2,1,0:T(2,128)(2,1)S(1)}, u32[]{:S(2)}, u32[]{:S(2)}) async-start(bf16[16,1,18]{2,1,0:T(2,128)(2,1)} %select_n.66), calls=%async_computation | async-start | bytes 16384 | tf_op jit(solution)/shard_map/all_to_all | solution.py:44
  22.3 3.0 copy-start.2
  33.5 28.7 %all-to-all-start.2 = ((bf16[16,18,2048]{2,1,0:T(8,128)(2,1)}), bf16[16,18,2048]{2,1,0:T(8,128)(2,1)}, u32[]{:S(2)}, u32[]{:S(2)}) async-start(bf16[16,18,2048]{2,1,0:T(8,128)(2,1)} %reshape.144), calls=%async_computation.2 | async-start | bytes 3145728 | tf_op jit(solution)/shard_map/all_to_all | solution.py:34
  62.2 28.1 %all-to-all-start.1 = ((bf16[16,18,2048]{2,1,0:T(8,128)(2,1)}), bf16[16,18,2048]{2,1,0:T(8,128)(2,1)}, u32[]{:S(2)}, u32[]{:S(2)}) async-start(bf16[16,18,2048]{2,1,0:T(8,128)(2,1)} %reshape.143), calls=%async_computation.1 | async-start | bytes 3145728 | tf_op jit(solution)/shard_map/all_to_all | solution.py:43
  68.8 313.2 %reduce-scatter.2.cloned.1.call-start = ((), (), s32[]{:S(2)}) async-start(), calls=%async_computation.5 | async-start | bytes 4259840 | tf_op jit(solution)/shard_map/reduce_scatter | solution.py:74
  71.3 2.2 copy-start.4
  71.3 2.3 copy-start.6
  73.5 32.5 %copy-start.3 = (f32[288,512]{1,0:T(8,128)}, f32[288,512]{1,0:T(8,128)S(1)}, u32[]{:S(2)}) copy-start(f32[288,512]{1,0:T(8,128)S(1)} %fusion.3) | copy-start | bytes 1769476
  106.1 1.6 copy-start.5
  111.0 6.9 %copy-start.7 = (s32[128,2]{0,1:T(2,128)S(1)}, s32[128,2]{0,1:T(2,128)}, u32[]{:S(2)}) copy-start(s32[128,2]{0,1:T(2,128)} %param.11) | copy-start | bytes 3076
  111.0 28.2 %all-to-all-start.3 = ((bf16[16,18,2048]{2,1,0:T(8,128)(2,1)}), bf16[16,18,2048]{2,1,0:T(8,128)(2,1)}, u32[]{:S(2)}, u32[]{:S(2)}) async-start(bf16[16,18,2048]{2,1,0:T(8,128)(2,1)} %reshape.146), calls=%async_computation.3 | async-start | bytes 3145728 | tf_op jit(solution)/shard_map/all_to_all | solution.py:63
Sparse Core Ops, SparseCore 0:
  98.1 283.8 reduce-scatter.1
where the time goes:
time: 390 us; the launch traced here: 389 us
  waiting for transfers between devices  291 us (75%)
  local copies, waits for them, and re-layouts  32.2 us (8%)
  starting transfers between devices  27 us (7%)
  between operations  14.3 us (4%)
  matrix products  13.5 us (3%)
  other arithmetic  10.6 us (3%)
    reduce_scatter x1, waiting for transfers between devices, body(): lax.psum_scatter(lax.dot_general(hidden, scaled, (((0,), (0,)), ((), ()))...  234 us
    all_to_all x1, waiting for transfers between devices, body(): lax.all_to_all(row_grads.reshape(experts_here, capacity, model_width), 'e...  21.1 us
    all_to_all x1, waiting for transfers between devices, body(): lax.all_to_all(sent_rows, 'expert', split_axis=0, concat_axis=0, tiled=True)  20.1 us
    all_to_all x1, waiting for transfers between devices, body(): lax.all_to_all(sent_grads, 'expert', split_axis=0, concat_axis=0, tiled=T...  15.9 us
  transfers between devices with their start and end apart: 5, of which 4 were waited for; matrix products, arithmetic and copies ran while one was open for 10% of the time, Pallas kernels for 0%

commit v1 on v0

v1 whole, which is shorter than its diff:
```python
import functools

import jax
import jax.numpy as jnp
from jax import lax
from jax.experimental import pallas as pl
from jax.experimental.pallas import tpu as pltpu
from jax.sharding import PartitionSpec as P

MESH = pl.DeviceIdType.MESH
F32, BF16 = jnp.float32, jnp.bfloat16
NT = (((1,), (1,)), ((), ()))
OFFSETS = (
    (2, 1, 0), (1, 0, 0), (3, 1, 0), (2, 0, 1), (1, 1, 1), (3, 0, 0), (0, 1, 0), (2, 0, 0),
    (1, 0, 1), (3, 1, 1), (2, 1, 1), (1, 1, 0), (3, 0, 1), (0, 1, 1), (0, 0, 1),
)


def nn(a, b):
    return jnp.dot(a, b, preferred_element_type=F32)


def nt(a, b):
    return lax.dot_general(a, b, NT, preferred_element_type=F32)


def kernel(
    nz, nx,
    tok, cot, ids, gates, wg_hbm, wu_hbm, wd_hbm,
    out_tok, out_down,
    wg, wu, wd, xs, xr, sd, sr, rd, rr, sel, selt, perm, hid, hidt, act, mix, hb, gb, ub,
    part, psend, precv, rsend, rrecv, fin, ybuf,
    wsem, lsem, ssem, rsem, psem, prsem, gsem, grsem, ysem,
):
    toks, width = tok.shape
    half = width // 2
    lanes = 128
    cols = half // lanes
    experts = nx * 4
    main, more = 16 * experts, 2 * experts
    rows = main + more
    hidden = wg.shape[1]
    dp, me = lax.axis_index("dp"), lax.axis_index("expert")
    yl, z = dp // nz, dp % nz
    x, yh, c = me // 4, (me // 2) % 2, me % 2

    def at(z2):
        return (yl * nz + z2 % nz, me)

    peers = []
    for dx, dy, dc in OFFSETS:
        if dx < nx:
            x2, yh2, c2, yl2 = (x + dx) % nx, (yh + dy) % 2, (c + dc) % 2, (yl + dy) % 2
            e2 = x2 * 4 + yh2 * 2 + c2
            peers.append(((yl2 * nz + z, e2), e2))
    odd = z % 2
    pairs = ((z + 1 - 2 * odd), (z + nz - 1 + 2 * odd) % nz)
    up, down = at(z + 2), at(z + nz - 2)
    across = ((1 - yl) * nz + z, me)

    barrier = pltpu.get_barrier_semaphore()
    greet = [p[0] for p in peers] + [at(p) for p in pairs] + [up, down, across]
    for d in greet:
        pl.semaphore_signal(barrier, inc=1, device_id=d, device_id_type=MESH)

    loads = [
        pltpu.make_async_copy(a, b, wsem.at[i])
        for i, (a, b) in enumerate(((wg_hbm, wg), (wu_hbm, wu), (wd_hbm, wd)))
    ]
    for load in loads:
        load.start()

    def iota(shape, dim):
        return lax.broadcasted_iota(jnp.int32, shape, dim)

    eye = iota((toks, toks), 0) == iota((toks, toks), 1)
    before = (iota((toks, toks), 0) < iota((toks, toks), 1)).astype(F32).astype(BF16)
    idv = ids[...].astype(F32)
    gtv = gates[...].astype(F32)

    def as_row(v):
        return jnp.sum(jnp.where(eye, v, 0.0), axis=0, keepdims=True)

    id_rows = [as_row(idv[:, k : k + 1]) for k in (0, 1)]
    gate_rows = [as_row(gtv[:, k : k + 1]) for k in (0, 1)]
    named = [(iota((experts, toks), 0).astype(F32) == r).astype(F32) for r in id_rows]
    earlier = nn((named[0] + named[1]).astype(BF16), before)
    slot = iota((rows, toks), 0).astype(F32)
    picks = []
    for k in (0, 1):
        pos = jnp.sum(named[k] * earlier, axis=0, keepdims=True)
        target = jnp.where(pos < 16.0, id_rows[k] * 16.0 + pos, main + id_rows[k] * 2.0 + (pos - 16.0))
        picks.append((slot == target).astype(F32))
    sel[...] = (picks[0] + picks[1]).astype(BF16)
    slot_gates = jnp.sum(picks[0] * gate_rows[0] + picks[1] * gate_rows[1], axis=1, keepdims=True)
    r0, r1 = iota((main, main), 0), iota((main, main), 1)
    perm[...] = (r1 == (r0 % cols) * more + r0 // cols).astype(F32).astype(BF16)

    def pack(buf, h):
        tall = jnp.concatenate(
            [buf[h, main:rows, j * lanes : (j + 1) * lanes] for j in range(cols)], axis=0
        )
        buf[h, 0:main, half : half + lanes] = nn(perm[...], tall).astype(BF16)

    def unpack(buf, h):
        tall = lax.dot_general(
            perm[...], buf[h, 0:main, half : half + lanes], (((0,), (0,)), ((), ())),
            preferred_element_type=F32,
        ).astype(BF16)
        for j in range(cols):
            buf[h, main:rows, j * lanes : (j + 1) * lanes] = tall[j * more : (j + 1) * more]

    def gather(src, buf, h, scale):
        def tile(t, carry):
            lo = pl.multiple_of(t * 256, 256)
            v = nn(sel[...], src[:, pl.ds(pl.multiple_of(h * half + lo, 256), 256)])
            if scale is not None:
                v = v * scale
            buf[h, 0:rows, pl.ds(lo, 256)] = v.astype(BF16)
            return carry

        lax.fori_loop(0, half // 256, tile, 0)
        pack(buf, h)

    def swap(unit, src, dst, h):
        mine = pl.ds(pl.multiple_of(me * 16, 16), 16)
        copies = [
            pltpu.make_async_remote_copy(
                src_ref=src.at[h, pl.ds(pl.multiple_of(e2 * 16, 16), 16)],
                dst_ref=dst.at[h, mine],
                send_sem=ssem.at[unit, i], recv_sem=rsem.at[unit, i],
                device_id=dev, device_id_type=MESH,
            )
            for i, (dev, e2) in enumerate(peers)
        ]
        own = pltpu.make_async_copy(src.at[h, mine], dst.at[h, mine], lsem.at[unit])
        return copies, own

    swaps = [
        swap(0, xs, xr, 0), swap(1, xs, xr, 1), swap(2, sd, sr, 0), swap(3, sd, sr, 1),
        swap(4, rd, rr, 0), swap(5, rd, rr, 1),
    ]

    def send(unit):
        copies, own = swaps[unit]
        for copy in copies:
            copy.start()
        own.start()

    def arrive(unit):
        copies, own = swaps[unit]
        for copy in copies:
            copy.wait_recv()
        own.wait()

    gather(tok, xs, 0, None)
    pl.semaphore_wait(barrier, len(greet))
    send(0)
    gather(tok, xs, 1, None)
    send(1)
    gather(cot, sd, 0, slot_gates)
    send(2)
    gather(cot, sd, 1, slot_gates)
    send(3)

    selt[...] = nt(eye.astype(F32).astype(BF16), sel[...]).astype(BF16)
    loads[0].wait()
    loads[1].wait()
    arrive(0)
    arrive(1)
    unpack(xr, 0)
    unpack(xr, 1)

    tile_f = min(256, hidden)

    def first(t, carry):
        f = pl.ds(pl.multiple_of(t * tile_f, tile_f), tile_f)
        gate = nn(xr[0, 0:rows, 0:half], wg[0:half, f]) + nn(xr[1, 0:rows, 0:half], wg[half:width, f])
        upv = nn(xr[0, 0:rows, 0:half], wu[0:half, f]) + nn(xr[1, 0:rows, 0:half], wu[half:width, f])
        s = jax.nn.sigmoid(gate)
        a = gate * s
        hid[:, f] = (a * upv).astype(BF16)
        act[:, f] = a
        mix[:, f] = upv * s * (1.0 + gate * (1.0 - s))
        return carry

    lax.fori_loop(0, hidden // tile_f, first, 0)

    def turn(t, carry):
        lo = pl.multiple_of(t * tile_f, tile_f)
        to = lo + iota((tile_f, hidden), 0)
        par, rest = to // (hidden // 2), to % (hidden // 2)
        zz, low = (rest // 16) * 2 + par, rest % 16
        source = ((low // 8) * nz + zz) * 8 + low % 8
        move = (iota((tile_f, hidden), 1) == source).astype(F32).astype(BF16)
        hidt[pl.ds(lo, tile_f), :] = nt(move, hid[...]).astype(BF16)
        return carry

    lax.fori_loop(0, hidden // tile_f, turn, 0)
    loads[2].wait()

    nodes = nz // 2
    a_mine = z // 2
    steps_up, steps_down = nodes // 2, nodes // 2 - 1

    def chunk(par, a):
        return pl.ds(pl.multiple_of(par * (hidden // 2) + (a % nodes) * 16, 16), 16)

    def order(a):
        found = []
        for k in range(steps_up):
            found.append((a + nodes // 2 - k, "up", k))
            if k < steps_down:
                found.append((a + nodes - steps_down + k, "down", k))
        return found + [(a, "own", 0)]

    def pair_copies(h):
        partner = pairs[h]
        copies = []
        for j, (a, _, _) in enumerate(order(partner // 2)):
            slot_j = pl.ds(j * 16, 16)
            copies.append(
                pltpu.make_async_remote_copy(
                    src_ref=psend.at[h, slot_j], dst_ref=precv.at[h, slot_j],
                    send_sem=psem.at[h, j], recv_sem=prsem.at[h, j],
                    device_id=at(partner), device_id_type=MESH,
                )
            )
        return copies

    pair = [pair_copies(0), pair_copies(1)]
    mine = {(way, k): (j, a) for j, (a, way, k) in enumerate(order(a_mine))}

    def products(h):
        def tile(t, carry):
            lo = pl.ds(pl.multiple_of(t * 256, 256), 256)
            part[h, :, lo] = nn(hidt[...], sr[h, 0:rows, lo])
            return carry

        lax.fori_loop(0, half // 256, tile, 0)
        for j, (a, _, _) in enumerate(order(pairs[h] // 2)):
            psend[h, j * 16 : (j + 1) * 16] = part[h, chunk(1 - odd, a), :].astype(BF16)
            pair[h][j].start()

        def back(t, carry):
            f = pl.ds(pl.multiple_of(t * tile_f, tile_f), tile_f)
            v = nt(sr[h, 0:rows, 0:half], wd[f, h * half : (h + 1) * half])
            hb[:, f] = v if h == 0 else hb[:, f] + v
            return carry

        lax.fori_loop(0, hidden // tile_f, back, 0)

    def ring_copy(h, way, k):
        d = 0 if way == "up" else 1
        span = pl.ds(k * 16, 16)
        return pltpu.make_async_remote_copy(
            src_ref=rsend.at[d, h, span], dst_ref=rrecv.at[d, h, span],
            send_sem=gsem.at[d, h, k], recv_sem=grsem.at[d, h, k],
            device_id=up if way == "up" else down, device_id_type=MESH,
        )

    def own_sum(h, way, k):
        j, a = mine[way, k]
        pair[h][j].wait_recv()
        return part[h, chunk(odd, a), :] + precv[h, j * 16 : (j + 1) * 16].astype(F32)

    def ring_step(k):
        for h in (0, 1):
            for d, (way, steps) in enumerate((("up", steps_up), ("down", steps_down))):
                if k < steps:
                    v = own_sum(h, way, k)
                    if k > 0:
                        ring_copy(h, way, k - 1).wait_recv()
                        v = v + rrecv[d, h, (k - 1) * 16 : k * 16].astype(F32)
                    rsend[d, h, k * 16 : (k + 1) * 16] = v.astype(BF16)
                    ring_copy(h, way, k).start()

    arrive(2)
    unpack(sr, 0)
    products(0)
    arrive(3)
    unpack(sr, 1)
    products(1)

    gb[...] = (hb[...] * mix[...]).astype(BF16)
    ub[...] = (hb[...] * act[...]).astype(BF16)

    def row_grads(h):
        def tile(t, carry):
            lo = pl.multiple_of(t * 256, 256)
            w = pl.ds(pl.multiple_of(h * half + lo, 256), 256)
            rd[h, 0:rows, pl.ds(lo, 256)] = (nt(gb[...], wg[w, :]) + nt(ub[...], wu[w, :])).astype(BF16)
            return carry

        lax.fori_loop(0, half // 256, tile, 0)
        pack(rd, h)

    def combine(h):
        unpack(rr, h)

        def tile(t, carry):
            lo = pl.multiple_of(t * 256, 256)
            w = pl.ds(pl.multiple_of(h * half + lo, 256), 256)
            out_tok[:, w] = nn(selt[...], rr[h, 0:rows, pl.ds(lo, 256)]).astype(BF16)
            return carry

        lax.fori_loop(0, half // 256, tile, 0)

    row_grads(0)
    send(4)
    ring_step(0)
    row_grads(1)
    send(5)
    for k in range(1, steps_up):
        ring_step(k)

    for h in (0, 1):
        v = own_sum(h, "own", 0)
        for d, (way, steps) in enumerate((("up", steps_up), ("down", steps_down))):
            if steps > 0:
                ring_copy(h, way, steps - 1).wait_recv()
                v = v + rrecv[d, h, (steps - 1) * 16 : steps * 16].astype(F32)
        fin[:, h * half : (h + 1) * half] = v
    last = pltpu.make_async_remote_copy(
        src_ref=fin.at[pl.ds(pl.multiple_of((1 - yl) * 8, 8), 8)], dst_ref=ybuf,
        send_sem=ysem.at[0], recv_sem=ysem.at[1], device_id=across, device_id_type=MESH,
    )
    last.start()
    for h in (0, 1):
        arrive(4 + h)
        combine(h)
    last.wait_recv()
    out_down[...] = fin[pl.ds(pl.multiple_of(yl * 8, 8), 8), :] + ybuf[...]

    last.wait_send()
    for copies, _ in swaps:
        for copy in copies:
            copy.wait_send()
    for h in (0, 1):
        for copy in pair[h]:
            copy.wait_send()
        for way, steps in (("up", steps_up), ("down", steps_down)):
            for k in range(steps):
                ring_copy(h, way, k).wait_send()


def solution(mesh):
    nz, experts = mesh.shape["dp"] // 2, mesh.shape["expert"]

    def body(tokens, cotangent, expert_ids, gate_values, gate_weights, up_weights, down_weights):
        toks, width = tokens.shape
        hidden = gate_weights.shape[2]
        half, rows, main = width // 2, 18 * experts, 16 * experts
        n = experts - 1
        nodes = nz // 2
        vmem = pl.BlockSpec(memory_space=pltpu.VMEM)
        hbm = pl.BlockSpec(memory_space=pl.ANY)
        block = pltpu.VMEM((2, rows, half + 128), BF16)
        dma = pltpu.SemaphoreType.DMA
        flops = 2 * rows * width * hidden * 6
        out_tok, out_down = pl.pallas_call(
            functools.partial(kernel, nz, experts // 4),
            out_shape=(
                jax.ShapeDtypeStruct((toks, width), BF16),
                jax.ShapeDtypeStruct((8, width), F32),
            ),
            in_specs=[vmem] * 4 + [hbm] * 3,
            out_specs=(vmem, vmem),
            scratch_shapes=[
                pltpu.VMEM((width, hidden), BF16), pltpu.VMEM((width, hidden), BF16), pltpu.VMEM((hidden, width), BF16),
                block, block, block, block, block, block,
                pltpu.VMEM((rows, toks), BF16), pltpu.VMEM((toks, rows), BF16), pltpu.VMEM((main, main), BF16),
                pltpu.VMEM((rows, hidden), BF16), pltpu.VMEM((hidden, rows), BF16),
                pltpu.VMEM((rows, hidden), F32), pltpu.VMEM((rows, hidden), F32), pltpu.VMEM((rows, hidden), F32),
                pltpu.VMEM((rows, hidden), BF16), pltpu.VMEM((rows, hidden), BF16),
                pltpu.VMEM((2, hidden, half), F32),
                pltpu.VMEM((2, nodes * 16, half), BF16), pltpu.VMEM((2, nodes * 16, half), BF16),
                pltpu.VMEM((2, 2, nodes // 2 * 16, half), BF16), pltpu.VMEM((2, 2, nodes // 2 * 16, half), BF16),
                pltpu.VMEM((16, width), F32), pltpu.VMEM((8, width), F32),
                dma((3,)), dma((6,)), dma((6, n)), dma((6, n)),
                dma((2, nodes)), dma((2, nodes)), dma((2, 2, nodes // 2)), dma((2, 2, nodes // 2)), dma((2,)),
            ],
            compiler_params=pltpu.CompilerParams(
                collective_id=0, has_side_effects=True, vmem_limit_bytes=52 * 2**20
            ),
            cost_estimate=pl.CostEstimate(flops=flops, bytes_accessed=8 * 2**20, transcendentals=rows * hidden),
        )(tokens, cotangent, expert_ids, gate_values, gate_weights[0], up_weights[0], down_weights[0])
        return out_tok, out_down[None]

    return jax.shard_map(
        body,
        mesh=mesh,
        in_specs=(
            P(("dp", "expert"), None),
            P(("dp", "expert"), None),
            P(("dp", "expert"), None),
            P(("dp", "expert"), None),
            P("expert", None, None),
            P("expert", None, None),
            P("expert", None, None),
        ),
        out_specs=(P(("dp", "expert"), None), P("expert", "dp", None)),
        check_vma=False,
    )
```

time: 390 us -> 110 us (0.28)
  the two profiles are of different devices: /device:TPU:12 before, /device:TPU:118 now
where the time goes in v1:
time: 110 us; the launch traced here: 109 us
  Pallas kernels  104 us (95%)
  local copies, waits for them, and re-layouts  5.07 us (5%)
    pallas_call x1, Pallas kernels, body(): pl.pallas_call(functools.partial(kernel, nz, experts // 4), out_shape=(ja...  104 us
    unnamed x8, local copies, waits for them, and re-layouts  5.07 us

profile of v1, /device:TPU:118, one launch (start us, length us, event | category | flops | bytes accessed | tf_op | source)
XLA Modules:
  0.0 109.3 jit_solution(4364462221685335263)
XLA Ops:
  0.6 0.8 copy.10.gates
  1.4 0.8 copy.9.ids
  2.2 0.0 copy-start
  2.2 1.0 copy-done
  3.2 0.0 copy-start.1
  3.2 1.0 copy-done.1
  4.3 103.5 %shard_map.86 = (bf16[128,2048]{1,0:T(8,128)(2,1)S(1)}, f32[8,2048]{1,0:T(8,128)S(1)}) custom-call(bf16[128,2048]{1,0:T(8,128)(2,1)S(1)} %copy-done, bf16[128,2048]{1,0:T(8,128)(2,1)S(1)} %copy-done.1, s32[128,2]{1,0:T(8,128)S(1)} %copy.9.ids, bf16[128,2]{1,0:T(8,128)(2,1)S(1)} %copy.10.gates, bf16[2048,512]{1,0:T(8,128)(2,1)} %bitcast.5, ...), custom_call_target="tpu_custom_call" | custom-call | flops 3623878656 | bytes 8388608 | tf_op jit(solution)/shard_map/pallas_call | solution.py:361
  107.8 0.8 copy.13
  108.6 0.6 copy.14
Async XLA Ops:
  2.2 1.0 copy-start
  3.2 1.0 copy-start.1

commit v2 on v1

--- a/solution.py
+++ b/solution.py
@@ -11,8 +11,8 @@
 F32, BF16 = jnp.float32, jnp.bfloat16
 NT = (((1,), (1,)), ((), ()))
 OFFSETS = (
-    (2, 1, 0), (1, 0, 0), (3, 1, 0), (2, 0, 1), (1, 1, 1), (3, 0, 0), (0, 1, 0), (2, 0, 0),
-    (1, 0, 1), (3, 1, 1), (2, 1, 1), (1, 1, 0), (3, 0, 1), (0, 1, 1), (0, 0, 1),
+    (2, 1, 0), (2, 1, 1), (3, 1, 0), (2, 0, 0), (1, 1, 0), (2, 0, 1), (1, 1, 1), (3, 1, 1),
+    (1, 0, 0), (3, 0, 0), (0, 1, 0), (1, 0, 1), (3, 0, 1), (0, 1, 1), (0, 0, 1),
 )
 
 
@@ -26,11 +26,11 @@
 
 def kernel(
     nz, nx,
-    tok, cot, ids, gates, wg_hbm, wu_hbm, wd_hbm,
+    tok_hbm, cot_hbm, ids, gates, wg_hbm, wu_hbm, wd_hbm,
     out_tok, out_down,
-    wg, wu, wd, xs, xr, sd, sr, rd, rr, sel, selt, perm, hid, hidt, act, mix, hb, gb, ub,
-    part, psend, precv, rsend, rrecv, fin, ybuf,
-    wsem, lsem, ssem, rsem, psem, prsem, gsem, grsem, ysem,
+    tok, cot, wg, wu, wd, xs, xr, sd, sr, rd, rr, sel, selt, perm, hid, hidt, act, mix, hb, gb, ub,
+    part, psend, precv, rsend, rrecv, fsend, frecv, fin, ybuf,
+    wsem, lsem, ssem, rsem, psem, prsem, gsem, grsem, fsem, frsem, ysem,
 ):
     toks, width = tok.shape
     half = width // 2
@@ -44,8 +44,8 @@
     yl, z = dp // nz, dp % nz
     x, yh, c = me // 4, (me // 2) % 2, me % 2
 
-    def at(z2):
-        return (yl * nz + z2 % nz, me)
+    def at(z2, y2=None):
+        return ((yl if y2 is None else y2) * nz + z2 % nz, me)
 
     peers = []
     for dx, dy, dc in OFFSETS:
@@ -60,12 +60,15 @@
 
     barrier = pltpu.get_barrier_semaphore()
     greet = [p[0] for p in peers] + [at(p) for p in pairs] + [up, down, across]
+    greet += [at(z + 2, 1 - yl), at(z + nz - 2, 1 - yl)]
     for d in greet:
         pl.semaphore_signal(barrier, inc=1, device_id=d, device_id_type=MESH)
 
     loads = [
         pltpu.make_async_copy(a, b, wsem.at[i])
-        for i, (a, b) in enumerate(((wg_hbm, wg), (wu_hbm, wu), (wd_hbm, wd)))
+        for i, (a, b) in enumerate(
+            ((tok_hbm, tok), (cot_hbm, cot), (wg_hbm, wg), (wu_hbm, wu), (wd_hbm, wd))
+        )
     ]
     for load in loads:
         load.start()
@@ -78,11 +81,8 @@
     idv = ids[...].astype(F32)
     gtv = gates[...].astype(F32)
 
-    def as_row(v):
-        return jnp.sum(jnp.where(eye, v, 0.0), axis=0, keepdims=True)
-
-    id_rows = [as_row(idv[:, k : k + 1]) for k in (0, 1)]
-    gate_rows = [as_row(gtv[:, k : k + 1]) for k in (0, 1)]
+    id_rows = [idv[k : k + 1] for k in (0, 1)]
+    gate_rows = [gtv[k : k + 1] for k in (0, 1)]
     named = [(iota((experts, toks), 0).astype(F32) == r).astype(F32) for r in id_rows]
     earlier = nn((named[0] + named[1]).astype(BF16), before)
     slot = iota((rows, toks), 0).astype(F32)
@@ -153,19 +153,21 @@
             copy.wait_recv()
         own.wait()
 
+    loads[0].wait()
     gather(tok, xs, 0, None)
     pl.semaphore_wait(barrier, len(greet))
     send(0)
     gather(tok, xs, 1, None)
     send(1)
+    loads[1].wait()
     gather(cot, sd, 0, slot_gates)
     send(2)
     gather(cot, sd, 1, slot_gates)
     send(3)
 
     selt[...] = nt(eye.astype(F32).astype(BF16), sel[...]).astype(BF16)
-    loads[0].wait()
-    loads[1].wait()
+    loads[2].wait()
+    loads[3].wait()
     arrive(0)
     arrive(1)
     unpack(xr, 0)
@@ -197,7 +199,7 @@
         return carry
 
     lax.fori_loop(0, hidden // tile_f, turn, 0)
-    loads[2].wait()
+    loads[4].wait()
 
     nodes = nz // 2
     a_mine = z // 2
@@ -242,6 +244,7 @@
             psend[h, j * 16 : (j + 1) * 16] = part[h, chunk(1 - odd, a), :].astype(BF16)
             pair[h][j].start()
 
+    def backward(h):
         def back(t, carry):
             f = pl.ds(pl.multiple_of(t * tile_f, tile_f), tile_f)
             v = nt(sr[h, 0:rows, 0:half], wd[f, h * half : (h + 1) * half])
@@ -264,26 +267,39 @@
         pair[h][j].wait_recv()
         return part[h, chunk(odd, a), :] + precv[h, j * 16 : (j + 1) * 16].astype(F32)
 
-    def ring_step(k):
-        for h in (0, 1):
-            for d, (way, steps) in enumerate((("up", steps_up), ("down", steps_down))):
-                if k < steps:
-                    v = own_sum(h, way, k)
-                    if k > 0:
-                        ring_copy(h, way, k - 1).wait_recv()
-                        v = v + rrecv[d, h, (k - 1) * 16 : k * 16].astype(F32)
+    ways = (("up", steps_up), ("down", steps_down))
+
+    def final_copy(h, d, piece):
+        to = z + 2 if d == 0 else z + nz - 2
+        return pltpu.make_async_remote_copy(
+            src_ref=fsend.at[d, h, piece], dst_ref=frecv.at[d, h, yl],
+            send_sem=fsem.at[d, h, piece], recv_sem=frsem.at[d, h, yl],
+            device_id=at(to, piece), device_id_type=MESH,
+        )
+
+    def final_arrival(h, d, source):
+        return pltpu.make_async_remote_copy(
+            src_ref=fsend.at[d, h, source], dst_ref=frecv.at[d, h, source],
+            send_sem=fsem.at[d, h, source], recv_sem=frsem.at[d, h, source],
+            device_id=up, device_id_type=MESH,
+        )
+
+    def ring_step(h, k):
+        for d, (way, steps) in enumerate(ways):
+            if k < steps:
+                v = own_sum(h, way, k)
+                if k > 0:
+                    ring_copy(h, way, k - 1).wait_recv()
+                    v = v + rrecv[d, h, (k - 1) * 16 : k * 16].astype(F32)
+                if k < steps - 1:
                     rsend[d, h, k * 16 : (k + 1) * 16] = v.astype(BF16)
                     ring_copy(h, way, k).start()
-
-    arrive(2)
-    unpack(sr, 0)
-    products(0)
-    arrive(3)
-    unpack(sr, 1)
-    products(1)
-
-    gb[...] = (hb[...] * mix[...]).astype(BF16)
-    ub[...] = (hb[...] * act[...]).astype(BF16)
+                else:
+                    for piece in (0, 1):
+                        top = v[piece * 8 : (piece + 1) * 8]
+                        folded = jnp.concatenate([top[:, : half // 2], top[:, half // 2 :]], axis=0)
+                        fsend[d, h, piece] = folded.astype(BF16)
+                        final_copy(h, d, piece).start()
 
     def row_grads(h):
         def tile(t, carry):
@@ -306,31 +322,52 @@
 
         lax.fori_loop(0, half // 256, tile, 0)
 
-    row_grads(0)
-    send(4)
-    ring_step(0)
-    row_grads(1)
-    send(5)
-    for k in range(1, steps_up):
-        ring_step(k)
-
-    for h in (0, 1):
-        v = own_sum(h, "own", 0)
-        for d, (way, steps) in enumerate((("up", steps_up), ("down", steps_down))):
-            if steps > 0:
-                ring_copy(h, way, steps - 1).wait_recv()
-                v = v + rrecv[d, h, (steps - 1) * 16 : steps * 16].astype(F32)
-        fin[:, h * half : (h + 1) * half] = v
     last = pltpu.make_async_remote_copy(
         src_ref=fin.at[pl.ds(pl.multiple_of((1 - yl) * 8, 8), 8)], dst_ref=ybuf,
         send_sem=ysem.at[0], recv_sem=ysem.at[1], device_id=across, device_id_type=MESH,
     )
-    last.start()
+
+    arrive(2)
+    unpack(sr, 0)
+    products(0)
+    backward(0)
+    ring_step(0, 0)
+    arrive(3)
+    unpack(sr, 1)
+    products(1)
+    ring_step(0, 1)
+    backward(1)
+    gb[...] = (hb[...] * mix[...]).astype(BF16)
+    ub[...] = (hb[...] * act[...]).astype(BF16)
+    row_grads(0)
+    send(4)
+    ring_step(1, 0)
+    ring_step(0, 2)
+    row_grads(1)
+    send(5)
+    for k in range(1, steps_up):
+        ring_step(1, k)
+        ring_step(0, k + 2)
+        if k == steps_up - 4:
+            for h in (0, 1):
+                fin[:, h * half : (h + 1) * half] = own_sum(h, "own", 0)
+            last.start()
+        if k >= steps_up - 2:
+            h = k - (steps_up - 2)
+            arrive(4 + h)
+            combine(h)
+
+    last.wait_recv()
+    kept = pl.ds(pl.multiple_of(yl * 8, 8), 8)
     for h in (0, 1):
-        arrive(4 + h)
-        combine(h)
-    last.wait_recv()
-    out_down[...] = fin[pl.ds(pl.multiple_of(yl * 8, 8), 8), :] + ybuf[...]
+        span = slice(h * half, (h + 1) * half)
+        v = fin[kept, span] + ybuf[:, span]
+        for d in (0, 1):
+            for source in (0, 1):
+                final_arrival(h, d, source).wait_recv()
+                piece = frecv[d, h, source].astype(F32)
+                v = v + jnp.concatenate([piece[0:8], piece[8:16]], axis=1)
+        out_down[:, span] = v
 
     last.wait_send()
     for copies, _ in swaps:
@@ -339,9 +376,11 @@
     for h in (0, 1):
         for copy in pair[h]:
             copy.wait_send()
-        for way, steps in (("up", steps_up), ("down", steps_down)):
-            for k in range(steps):
+        for d, (way, steps) in enumerate(ways):
+            for k in range(steps - 1):
                 ring_copy(h, way, k).wait_send()
+            for piece in (0, 1):
+                final_copy(h, d, piece).wait_send()
 
 
 def solution(mesh):
@@ -364,9 +403,10 @@
                 jax.ShapeDtypeStruct((toks, width), BF16),
                 jax.ShapeDtypeStruct((8, width), F32),
             ),
-            in_specs=[vmem] * 4 + [hbm] * 3,
+            in_specs=[hbm] * 2 + [vmem] * 2 + [hbm] * 3,
             out_specs=(vmem, vmem),
             scratch_shapes=[
+                pltpu.VMEM((toks, width), BF16), pltpu.VMEM((toks, width), BF16),
                 pltpu.VMEM((width, hidden), BF16), pltpu.VMEM((width, hidden), BF16), pltpu.VMEM((hidden, width), BF16),
                 block, block, block, block, block, block,
                 pltpu.VMEM((rows, toks), BF16), pltpu.VMEM((toks, rows), BF16), pltpu.VMEM((main, main), BF16),
@@ -376,15 +416,17 @@
                 pltpu.VMEM((2, hidden, half), F32),
                 pltpu.VMEM((2, nodes * 16, half), BF16), pltpu.VMEM((2, nodes * 16, half), BF16),
                 pltpu.VMEM((2, 2, nodes // 2 * 16, half), BF16), pltpu.VMEM((2, 2, nodes // 2 * 16, half), BF16),
+                pltpu.VMEM((2, 2, 2, 16, half // 2), BF16), pltpu.VMEM((2, 2, 2, 16, half // 2), BF16),
                 pltpu.VMEM((16, width), F32), pltpu.VMEM((8, width), F32),
-                dma((3,)), dma((6,)), dma((6, n)), dma((6, n)),
-                dma((2, nodes)), dma((2, nodes)), dma((2, 2, nodes // 2)), dma((2, 2, nodes // 2)), dma((2,)),
+                dma((5,)), dma((6,)), dma((6, n)), dma((6, n)),
+                dma((2, nodes)), dma((2, nodes)), dma((2, 2, nodes // 2)), dma((2, 2, nodes // 2)),
+                dma((2, 2, 2)), dma((2, 2, 2)), dma((2,)),
             ],
             compiler_params=pltpu.CompilerParams(
-                collective_id=0, has_side_effects=True, vmem_limit_bytes=52 * 2**20
+                collective_id=0, has_side_effects=True, vmem_limit_bytes=60 * 2**20
             ),
             cost_estimate=pl.CostEstimate(flops=flops, bytes_accessed=8 * 2**20, transcendentals=rows * hidden),
-        )(tokens, cotangent, expert_ids, gate_values, gate_weights[0], up_weights[0], down_weights[0])
+        )(tokens, cotangent, expert_ids.T, gate_values.T, gate_weights[0], up_weights[0], down_weights[0])
         return out_tok, out_down[None]
 
     return jax.shard_map(

time: 110 us -> 108 us (0.982)
  the two profiles are of different devices: /device:TPU:118 before, /device:TPU:32 now
where the time goes in v2:
time: 108 us
  Pallas kernels  104 us (96%)
  local copies, waits for them, and re-layouts  3.35 us (3%)
    pallas_call x1, Pallas kernels, body(): pl.pallas_call(functools.partial(kernel, nz, experts // 4), out_shape=(ja...  104 us
    unnamed x2, local copies, waits for them, and re-layouts  3.35 us

profile of v2, /device:TPU:32, one launch (start us, length us, event | category | flops | bytes accessed | tf_op | source)
XLA Modules:
  0.0 107.8 jit_solution(10471291478454806506)
XLA Ops:
  0.6 103.8 %shard_map.86 = (bf16[128,2048]{1,0:T(8,128)(2,1)}, f32[8,2048]{1,0:T(8,128)}) custom-call(bf16[128,2048]{1,0:T(8,128)(2,1)} %tok_hbm.1, bf16[128,2048]{1,0:T(8,128)(2,1)} %cot_hbm.1, s32[2,128]{1,0:T(2,128)} %bitcast.10, bf16[2,128]{1,0:T(2,128)(2,1)} %bitcast.11, bf16[2048,512]{1,0:T(8,128)(2,1)} %bitcast.7, bf16[2048,512]{1,0:T(8,128)(2,1)} %bitcast.8, ...), custom_call_target="tpu_custom_call" | custom-call | flops 3623878656 | bytes 8388608 | tf_op jit(solution)/shard_map/pallas_call | solution.py:400
  104.5 1.9 %copy.11 = bf16[128,2048]{1,0:T(8,128)(2,1)} copy(bf16[128,2048]{1,0:T(8,128)(2,1)} %get-tuple-element.8) | data formatting | bytes 1048576
  106.4 1.5 %copy.12 = f32[1,8,2048]{2,1,0:T(8,128)} copy(f32[1,8,2048]{2,1,0:T(8,128)} %bitcast.6) | data formatting | bytes 131072

commit v3 on v2

v3 whole, which is shorter than its diff:
```python
import functools

import jax
import jax.numpy as jnp
from jax import lax
from jax.experimental import pallas as pl
from jax.experimental.pallas import tpu as pltpu
from jax.sharding import PartitionSpec as P

MESH = pl.DeviceIdType.MESH
F32, BF16 = jnp.float32, jnp.bfloat16
NT = (((1,), (1,)), ((), ()))
OFFSETS = (
    (2, 1, 0), (2, 1, 1), (3, 1, 0), (2, 0, 0), (1, 1, 0), (2, 0, 1), (1, 1, 1), (3, 1, 1),
    (1, 0, 0), (3, 0, 0), (0, 1, 0), (1, 0, 1), (3, 0, 1), (0, 1, 1), (0, 0, 1),
)


def nn(a, b):
    return jnp.dot(a, b, preferred_element_type=F32)


def nt(a, b):
    return lax.dot_general(a, b, NT, preferred_element_type=F32)


def kernel(
    nz, nx,
    tok_hbm, cot_hbm, ids, gates, wg_hbm, wu_hbm, wd_hbm,
    out_tok, out_down,
    tok, cot, wg, wu, wd, xs, xr, sd, sr, rd, rr, sel, selt, perm, hid, hidt, act, mix, hb, gb, ub,
    part, ysend, yrecv, acc, zsend, zrecv, rsend, rrecv,
    wsem, lsem, ssem, rsem, ysem, yrsem, zsem, zrsem, gsem, grsem,
):
    toks, width = tok.shape
    half = width // 2
    lanes = 128
    cols = half // lanes
    experts = nx * 4
    main, more = 16 * experts, 2 * experts
    rows = main + more
    hidden = wg.shape[1]
    dp, me = lax.axis_index("dp"), lax.axis_index("expert")
    yl, z = dp // nz, dp % nz
    x, yh, c = me // 4, (me // 2) % 2, me % 2

    def at(z2):
        return (yl * nz + z2 % nz, me)

    peers = []
    for dx, dy, dc in OFFSETS:
        if dx < nx:
            x2, yh2, c2, yl2 = (x + dx) % nx, (yh + dy) % 2, (c + dc) % 2, (yl + dy) % 2
            e2 = x2 * 4 + yh2 * 2 + c2
            peers.append(((yl2 * nz + z, e2), e2))
    partners = [[z + nz - (z + 2 * h) % 4 + ((z + 2 * h) % 4 + t) % 4 for t in (1, 2, 3)] for h in (0, 1)]
    up, down = at(z + 4), at(z + nz - 4)
    across = ((1 - yl) * nz + z, me)

    barrier = pltpu.get_barrier_semaphore()
    greet = [p[0] for p in peers] + [at(p) for row in partners for p in row] + [up, down, across]
    for d in greet:
        pl.semaphore_signal(barrier, inc=1, device_id=d, device_id_type=MESH)

    loads = [
        pltpu.make_async_copy(a, b, wsem.at[i])
        for i, (a, b) in enumerate(
            ((tok_hbm, tok), (cot_hbm, cot), (wg_hbm, wg), (wu_hbm, wu), (wd_hbm, wd))
        )
    ]
    loads[0].start()
    loads[1].start()

    def iota(shape, dim):
        return lax.broadcasted_iota(jnp.int32, shape, dim)

    eye = iota((toks, toks), 0) == iota((toks, toks), 1)
    before = (iota((toks, toks), 0) < iota((toks, toks), 1)).astype(F32).astype(BF16)
    idv = ids[...].astype(F32)
    gtv = gates[...].astype(F32)

    id_rows = [idv[k : k + 1] for k in (0, 1)]
    gate_rows = [gtv[k : k + 1] for k in (0, 1)]
    named = [(iota((experts, toks), 0).astype(F32) == r).astype(F32) for r in id_rows]
    earlier = nn((named[0] + named[1]).astype(BF16), before)
    slot = iota((rows, toks), 0).astype(F32)
    picks = []
    for k in (0, 1):
        pos = jnp.sum(named[k] * earlier, axis=0, keepdims=True)
        target = jnp.where(pos < 16.0, id_rows[k] * 16.0 + pos, main + id_rows[k] * 2.0 + (pos - 16.0))
        picks.append((slot == target).astype(F32))
    sel[...] = (picks[0] + picks[1]).astype(BF16)
    r0, r1 = iota((main, main), 0), iota((main, main), 1)
    perm[...] = (r1 == (r0 % cols) * more + r0 // cols).astype(F32).astype(BF16)

    def pack(buf, h):
        tall = jnp.concatenate(
            [buf[h, main:rows, j * lanes : (j + 1) * lanes] for j in range(cols)], axis=0
        )
        buf[h, 0:main, half : half + lanes] = nn(perm[...], tall).astype(BF16)

    def unpack(buf, h):
        tall = lax.dot_general(
            perm[...], buf[h, 0:main, half : half + lanes], (((0,), (0,)), ((), ())),
            preferred_element_type=F32,
        ).astype(BF16)
        for j in range(cols):
            buf[h, main:rows, j * lanes : (j + 1) * lanes] = tall[j * more : (j + 1) * more]

    def gather(src, buf, h, scale):
        def tile(t, carry):
            lo = pl.multiple_of(t * 256, 256)
            v = nn(sel[...], src[:, pl.ds(pl.multiple_of(h * half + lo, 256), 256)])
            if scale is not None:
                v = v * scale
            buf[h, 0:rows, pl.ds(lo, 256)] = v.astype(BF16)
            return carry

        lax.fori_loop(0, half // 256, tile, 0, unroll=True)
        pack(buf, h)

    def swap(unit, src, dst, h):
        mine = pl.ds(pl.multiple_of(me * 16, 16), 16)
        copies = [
            pltpu.make_async_remote_copy(
                src_ref=src.at[h, pl.ds(pl.multiple_of(e2 * 16, 16), 16)],
                dst_ref=dst.at[h, mine],
                send_sem=ssem.at[unit, i], recv_sem=rsem.at[unit, i],
                device_id=dev, device_id_type=MESH,
            )
            for i, (dev, e2) in enumerate(peers)
        ]
        own = pltpu.make_async_copy(src.at[h, mine], dst.at[h, mine], lsem.at[unit])
        return copies, own

    swaps = [
        swap(0, xs, xr, 0), swap(1, xs, xr, 1), swap(2, sd, sr, 0), swap(3, sd, sr, 1),
        swap(4, rd, rr, 0), swap(5, rd, rr, 1),
    ]

    def send(unit):
        copies, own = swaps[unit]
        for copy in copies:
            copy.start()
        own.start()

    def arrive(unit):
        copies, own = swaps[unit]
        for copy in copies:
            copy.wait_recv()
        own.wait()

    loads[0].wait()
    gather(tok, xs, 0, None)
    pl.semaphore_wait(barrier, len(greet))
    send(0)
    gather(tok, xs, 1, None)
    send(1)
    for load in loads[2:]:
        load.start()
    slot_gates = jnp.sum(picks[0] * gate_rows[0] + picks[1] * gate_rows[1], axis=1, keepdims=True)
    loads[1].wait()
    gather(cot, sd, 0, slot_gates)
    send(2)
    gather(cot, sd, 1, slot_gates)
    send(3)

    selt[...] = nt(eye.astype(F32).astype(BF16), sel[...]).astype(BF16)
    loads[2].wait()
    loads[3].wait()
    arrive(0)
    arrive(1)
    unpack(xr, 0)
    unpack(xr, 1)

    tile_f = min(256, hidden)

    def first(t, carry):
        f = pl.ds(pl.multiple_of(t * tile_f, tile_f), tile_f)
        gate = nn(xr[0, 0:rows, 0:half], wg[0:half, f]) + nn(xr[1, 0:rows, 0:half], wg[half:width, f])
        upv = nn(xr[0, 0:rows, 0:half], wu[0:half, f]) + nn(xr[1, 0:rows, 0:half], wu[half:width, f])
        s = jax.nn.sigmoid(gate)
        a = gate * s
        hid[:, f] = (a * upv).astype(BF16)
        act[:, f] = a
        mix[:, f] = upv * s * (1.0 + gate * (1.0 - s))
        return carry

    lax.fori_loop(0, hidden // tile_f, first, 0)

    def turn(t, carry):
        lo = pl.multiple_of(t * tile_f, tile_f)
        move = (iota((tile_f, hidden), 1) == lo + iota((tile_f, hidden), 0)).astype(F32).astype(BF16)
        hidt[pl.ds(lo, tile_f), :] = nt(move, hid[...]).astype(BF16)
        return carry

    lax.fori_loop(0, hidden // tile_f, turn, 0)
    loads[4].wait()

    nodes = nz // 4
    node, place = z // 4, z % 4
    steps_up, steps_down = nodes // 2, nodes // 2 - 1
    order = []
    for k in range(steps_up):
        order.append((node + nodes // 2 - k) % nodes)
        if k < steps_down:
            order.append((node + nodes - steps_down + k) % nodes)
    order.append(node)
    quarter = half // 2

    def fold(v):
        return jnp.concatenate([v[:, :quarter], v[:, quarter:]], axis=0)

    def y_copy(h, j):
        span = pl.ds(j * 32, 32)
        return pltpu.make_async_remote_copy(
            src_ref=ysend.at[h, span], dst_ref=yrecv.at[h, span],
            send_sem=ysem.at[h, j], recv_sem=yrsem.at[h, j], device_id=across, device_id_type=MESH,
        )

    def z_copy(h, t, j):
        a = order[j]
        return pltpu.make_async_remote_copy(
            src_ref=zsend.at[h, t, pl.ds(j * 16, 16)],
            dst_ref=zrecv.at[h, t, pl.ds(pl.multiple_of(a * 16, 16), 16)],
            send_sem=zsem.at[h, t, j], recv_sem=zrsem.at[h, t, a],
            device_id=at(partners[h][t]), device_id_type=MESH,
        )

    def ring_copy(h, d, k):
        span = pl.ds(k * 16, 16)
        return pltpu.make_async_remote_copy(
            src_ref=rsend.at[d, h, span], dst_ref=rrecv.at[d, h, span],
            send_sem=gsem.at[d, h, k], recv_sem=grsem.at[d, h, k],
            device_id=(up, down)[d], device_id_type=MESH,
        )

    def group(y2, j):
        return pl.ds(pl.multiple_of(y2 * (hidden // 2) + order[j] * 32, 32), 32)

    def products(h):
        def tile(t, carry):
            lo = pl.ds(pl.multiple_of(t * 256, 256), 256)
            part[h, :, lo] = nn(hidt[...], sr[h, 0:rows, lo])
            return carry

        lax.fori_loop(0, half // 256, tile, 0)
        for j in range(nodes):
            ysend[h, j * 32 : (j + 1) * 32] = part[h, group(1 - yl, j), :].astype(BF16)
            y_copy(h, j).start()

    def run_of_four(h, j):
        y_copy(h, j).wait_recv()
        acc[h, j * 32 : (j + 1) * 32] = part[h, group(yl, j), :] + yrecv[h, j * 32 : (j + 1) * 32].astype(F32)
        for t in range(3):
            rows_of = pl.ds(pl.multiple_of(j * 32 + partners[h][t] % 4 * 8, 8), 8)
            zsend[h, t, j * 16 : (j + 1) * 16] = fold(acc[h, rows_of, :]).astype(BF16)
            z_copy(h, t, j).start()

    def sum_of_four(h, j):
        v = fold(acc[h, pl.ds(pl.multiple_of(j * 32 + place * 8, 8), 8), :])
        for t in range(3):
            z_copy(h, t, j).wait_recv()
            v = v + zrecv[h, t, pl.ds(pl.multiple_of(order[j] * 16, 16), 16), :].astype(F32)
        return v

    def ring_step(h, k):
        for d, steps in enumerate((steps_up, steps_down)):
            if k < steps:
                v = sum_of_four(h, 2 * k + d)
                if k > 0:
                    ring_copy(h, d, k - 1).wait_recv()
                    v = v + rrecv[d, h, (k - 1) * 16 : k * 16].astype(F32)
                rsend[d, h, k * 16 : (k + 1) * 16] = v.astype(BF16)
                ring_copy(h, d, k).start()

    def ring_end(h):
        v = sum_of_four(h, nodes - 1)
        for d, steps in enumerate((steps_up, steps_down)):
            ring_copy(h, d, steps - 1).wait_recv()
            v = v + rrecv[d, h, (steps - 1) * 16 : steps * 16].astype(F32)
        out_down[:, h * half : (h + 1) * half] = jnp.concatenate([v[0:8], v[8:16]], axis=1)

    def backward(h):
        def back(t, carry):
            f = pl.ds(pl.multiple_of(t * tile_f, tile_f), tile_f)
            v = nt(sr[h, 0:rows, 0:half], wd[f, h * half : (h + 1) * half])
            hb[:, f] = v if h == 0 else hb[:, f] + v
            return carry

        lax.fori_loop(0, hidden // tile_f, back, 0)

    def row_grads(h):
        def tile(t, carry):
            lo = pl.multiple_of(t * 256, 256)
            w = pl.ds(pl.multiple_of(h * half + lo, 256), 256)
            rd[h, 0:rows, pl.ds(lo, 256)] = (nt(gb[...], wg[w, :]) + nt(ub[...], wu[w, :])).astype(BF16)
            return carry

        lax.fori_loop(0, half // 256, tile, 0)
        pack(rd, h)

    def combine(h):
        unpack(rr, h)

        def tile(t, carry):
            lo = pl.multiple_of(t * 256, 256)
            w = pl.ds(pl.multiple_of(h * half + lo, 256), 256)
            out_tok[:, w] = nn(selt[...], rr[h, 0:rows, pl.ds(lo, 256)]).astype(BF16)
            return carry

        lax.fori_loop(0, half // 256, tile, 0)

    arrive(2)
    unpack(sr, 0)
    products(0)
    backward(0)
    run_of_four(0, 0)
    run_of_four(0, 1)
    arrive(3)
    unpack(sr, 1)
    products(1)
    run_of_four(0, 2)
    run_of_four(0, 3)
    ring_step(0, 0)
    backward(1)
    gb[...] = (hb[...] * mix[...]).astype(BF16)
    ub[...] = (hb[...] * act[...]).astype(BF16)
    row_grads(0)
    send(4)
    run_of_four(0, 4)
    run_of_four(0, 5)
    run_of_four(1, 0)
    run_of_four(1, 1)
    ring_step(0, 1)
    run_of_four(1, 2)
    run_of_four(1, 3)
    row_grads(1)
    send(5)
    ring_step(1, 0)
    run_of_four(0, 6)
    run_of_four(0, 7)
    ring_step(0, 2)
    run_of_four(1, 4)
    run_of_four(1, 5)
    ring_step(1, 1)
    ring_step(0, 3)
    run_of_four(1, 6)
    run_of_four(1, 7)
    ring_step(1, 2)
    arrive(4)
    combine(0)
    ring_step(1, 3)
    ring_end(0)
    arrive(5)
    combine(1)
    ring_end(1)

    for copies, _ in swaps:
        for copy in copies:
            copy.wait_send()
    for h in (0, 1):
        for j in range(nodes):
            y_copy(h, j).wait_send()
            for t in range(3):
                z_copy(h, t, j).wait_send()
        for d, steps in enumerate((steps_up, steps_down)):
            for k in range(steps):
                ring_copy(h, d, k).wait_send()


def solution(mesh):
    nz, experts = mesh.shape["dp"] // 2, mesh.shape["expert"]

    def body(tokens, cotangent, expert_ids, gate_values, gate_weights, up_weights, down_weights):
        toks, width = tokens.shape
        hidden = gate_weights.shape[2]
        half, rows, main = width // 2, 18 * experts, 16 * experts
        n = experts - 1
        nodes = nz // 4
        vmem = pl.BlockSpec(memory_space=pltpu.VMEM)
        hbm = pl.BlockSpec(memory_space=pl.ANY)
        block = pltpu.VMEM((2, rows, half + 128), BF16)
        dma = pltpu.SemaphoreType.DMA
        flops = 2 * rows * width * hidden * 6
        out_tok, out_down = pl.pallas_call(
            functools.partial(kernel, nz, experts // 4),
            out_shape=(
                pltpu.VMEM((toks, width), BF16),
                pltpu.VMEM((8, width), F32),
            ),
            in_specs=[hbm] * 2 + [vmem] * 2 + [hbm] * 3,
            out_specs=(vmem, vmem),
            scratch_shapes=[
                pltpu.VMEM((toks, width), BF16), pltpu.VMEM((toks, width), BF16),
                pltpu.VMEM((width, hidden), BF16), pltpu.VMEM((width, hidden), BF16), pltpu.VMEM((hidden, width), BF16),
                block, block, block, block, block, block,
                pltpu.VMEM((rows, toks), BF16), pltpu.VMEM((toks, rows), BF16), pltpu.VMEM((main, main), BF16),
                pltpu.VMEM((rows, hidden), BF16), pltpu.VMEM((hidden, rows), BF16),
                pltpu.VMEM((rows, hidden), F32), pltpu.VMEM((rows, hidden), F32), pltpu.VMEM((rows, hidden), F32),
                pltpu.VMEM((rows, hidden), BF16), pltpu.VMEM((rows, hidden), BF16),
                pltpu.VMEM((2, hidden, half), F32),
                pltpu.VMEM((2, nodes * 32, half), BF16), pltpu.VMEM((2, nodes * 32, half), BF16),
                pltpu.VMEM((2, nodes * 32, half), F32),
                pltpu.VMEM((2, 3, nodes * 16, half // 2), BF16), pltpu.VMEM((2, 3, nodes * 16, half // 2), BF16),
                pltpu.VMEM((2, 2, nodes // 2 * 16, half // 2), BF16), pltpu.VMEM((2, 2, nodes // 2 * 16, half // 2), BF16),
                dma((5,)), dma((6,)), dma((6, n)), dma((6, n)),
                dma((2, nodes)), dma((2, nodes)), dma((2, 3, nodes)), dma((2, 3, nodes)),
                dma((2, 2, nodes // 2)), dma((2, 2, nodes // 2)),
            ],
            compiler_params=pltpu.CompilerParams(
                collective_id=0, has_side_effects=True, vmem_limit_bytes=60 * 2**20
            ),
            cost_estimate=pl.CostEstimate(flops=flops, bytes_accessed=8 * 2**20, transcendentals=rows * hidden),
        )(tokens, cotangent, expert_ids.T, gate_values.T, gate_weights[0], up_weights[0], down_weights[0])
        return out_tok, out_down[None]

    return jax.shard_map(
        body,
        mesh=mesh,
        in_specs=(
            P(("dp", "expert"), None),
            P(("dp", "expert"), None),
            P(("dp", "expert"), None),
            P(("dp", "expert"), None),
            P("expert", None, None),
            P("expert", None, None),
            P("expert", None, None),
        ),
        out_specs=(P(("dp", "expert"), None), P("expert", "dp", None)),
        check_vma=False,
    )
```

time: 108 us -> 97.5 us (0.903)
  the two profiles are of different devices: /device:TPU:32 before, /device:TPU:78 now
where the time goes in v3:
time: 97.5 us; the launch traced here: 97.4 us
  Pallas kernels  95.3 us (98%)
  local copies, waits for them, and re-layouts  1.42 us (1%)
    pallas_call x1, Pallas kernels, body(): pl.pallas_call(functools.partial(kernel, nz, experts // 4), out_shape=(pl...  95.3 us

profile of v3, /device:TPU:78, one launch (start us, length us, event | category | flops | bytes accessed | tf_op | source)
XLA Modules:
  0.0 97.4 jit_solution(4391920230143347141)
XLA Ops:
  0.6 95.3 %shard_map.86 = (bf16[128,2048]{1,0:T(8,128)(2,1)S(1)}, f32[8,2048]{1,0:T(8,128)S(1)}) custom-call(bf16[128,2048]{1,0:T(8,128)(2,1)} %tok_hbm.1, bf16[128,2048]{1,0:T(8,128)(2,1)} %cot_hbm.1, s32[2,128]{1,0:T(2,128)} %bitcast.10, bf16[2,128]{1,0:T(2,128)(2,1)} %bitcast.11, bf16[2048,512]{1,0:T(8,128)(2,1)} %bitcast.7, bf16[2048,512]{1,0:T(8,128)(2,1)} %bitcast.8, ...), custom_call_target="tpu_custom_call" | custom-call | flops 3623878656 | bytes 8388608 | tf_op jit(solution)/shard_map/pallas_call | solution.py:386
  95.9 0.8 copy.11
  96.7 0.6 copy.12

commit v4 on v3

--- a/solution.py
+++ b/solution.py
@@ -53,7 +53,8 @@
             x2, yh2, c2, yl2 = (x + dx) % nx, (yh + dy) % 2, (c + dc) % 2, (yl + dy) % 2
             e2 = x2 * 4 + yh2 * 2 + c2
             peers.append(((yl2 * nz + z, e2), e2))
-    partners = [[z + nz - (z + 2 * h) % 4 + ((z + 2 * h) % 4 + t) % 4 for t in (1, 2, 3)] for h in (0, 1)]
+    places = [(z + 2 * h) % 4 for h in (0, 1)]
+    partners = [[z + nz - p + (p + t) % 4 for t in (1, 2, 3)] for p in places]
     up, down = at(z + 4), at(z + nz - 4)
     across = ((1 - yl) * nz + z, me)
 
@@ -198,14 +199,17 @@
     loads[4].wait()
 
     nodes = nz // 4
-    node, place = z // 4, z % 4
     steps_up, steps_down = nodes // 2, nodes // 2 - 1
-    order = []
-    for k in range(steps_up):
-        order.append((node + nodes // 2 - k) % nodes)
-        if k < steps_down:
-            order.append((node + nodes - steps_down + k) % nodes)
-    order.append(node)
+
+    def order_of(node):
+        found = []
+        for k in range(steps_up):
+            found.append((node + nodes // 2 - k) % nodes)
+            if k < steps_down:
+                found.append((node + nodes - steps_down + k) % nodes)
+        return found + [node]
+
+    orders = [order_of((z + 2 * h) % nz // 4) for h in (0, 1)]
     quarter = half // 2
 
     def fold(v):
@@ -219,11 +223,10 @@
         )
 
     def z_copy(h, t, j):
-        a = order[j]
+        span = pl.ds(j * 16, 16)
         return pltpu.make_async_remote_copy(
-            src_ref=zsend.at[h, t, pl.ds(j * 16, 16)],
-            dst_ref=zrecv.at[h, t, pl.ds(pl.multiple_of(a * 16, 16), 16)],
-            send_sem=zsem.at[h, t, j], recv_sem=zrsem.at[h, t, a],
+            src_ref=zsend.at[h, t, span], dst_ref=zrecv.at[h, t, span],
+            send_sem=zsem.at[h, t, j], recv_sem=zrsem.at[h, t, j],
             device_id=at(partners[h][t]), device_id_type=MESH,
         )
 
@@ -235,8 +238,12 @@
             device_id=(up, down)[d], device_id_type=MESH,
         )
 
-    def group(y2, j):
-        return pl.ds(pl.multiple_of(y2 * (hidden // 2) + order[j] * 32, 32), 32)
+    def group(h, y2, j):
+        found = []
+        for two in (0, 2):
+            row = y2 * (hidden // 2) + (orders[h][j] * 4 + nz - 2 * h + two) % nz * 8
+            found.append(part[h, pl.ds(pl.multiple_of(row, 16), 16), :])
+        return jnp.concatenate(found, axis=0)
 
     def products(h):
         def tile(t, carry):
@@ -245,23 +252,26 @@
             return carry
 
         lax.fori_loop(0, half // 256, tile, 0)
-        for j in range(nodes):
-            ysend[h, j * 32 : (j + 1) * 32] = part[h, group(1 - yl, j), :].astype(BF16)
+
+    def y_start(h, *js):
+        for j in js:
+            ysend[h, j * 32 : (j + 1) * 32] = group(h, 1 - yl, j).astype(BF16)
             y_copy(h, j).start()
 
-    def run_of_four(h, j):
-        y_copy(h, j).wait_recv()
-        acc[h, j * 32 : (j + 1) * 32] = part[h, group(yl, j), :] + yrecv[h, j * 32 : (j + 1) * 32].astype(F32)
-        for t in range(3):
-            rows_of = pl.ds(pl.multiple_of(j * 32 + partners[h][t] % 4 * 8, 8), 8)
-            zsend[h, t, j * 16 : (j + 1) * 16] = fold(acc[h, rows_of, :]).astype(BF16)
-            z_copy(h, t, j).start()
+    def run_of_four(h, *js):
+        for j in js:
+            y_copy(h, j).wait_recv()
+            acc[h, j * 32 : (j + 1) * 32] = group(h, yl, j) + yrecv[h, j * 32 : (j + 1) * 32].astype(F32)
+            for t in range(3):
+                rows_of = pl.ds(pl.multiple_of(j * 32 + (places[h] + t + 1) % 4 * 8, 8), 8)
+                zsend[h, t, j * 16 : (j + 1) * 16] = fold(acc[h, rows_of, :]).astype(BF16)
+                z_copy(h, t, j).start()
 
     def sum_of_four(h, j):
-        v = fold(acc[h, pl.ds(pl.multiple_of(j * 32 + place * 8, 8), 8), :])
+        v = fold(acc[h, pl.ds(pl.multiple_of(j * 32 + places[h] * 8, 8), 8), :])
         for t in range(3):
             z_copy(h, t, j).wait_recv()
-            v = v + zrecv[h, t, pl.ds(pl.multiple_of(order[j] * 16, 16), 16), :].astype(F32)
+            v = v + zrecv[h, t, j * 16 : (j + 1) * 16].astype(F32)
         return v
 
     def ring_step(h, k):
@@ -314,44 +324,42 @@
     arrive(2)
     unpack(sr, 0)
     products(0)
+    y_start(0, 0, 1, 2, 3)
     backward(0)
-    run_of_four(0, 0)
-    run_of_four(0, 1)
+    run_of_four(0, 0, 1)
     arrive(3)
     unpack(sr, 1)
     products(1)
-    run_of_four(0, 2)
-    run_of_four(0, 3)
-    ring_step(0, 0)
+    y_start(1, 0, 1)
+    y_start(0, 4, 5)
+    y_start(1, 2, 3)
+    y_start(0, 6, 7)
+    y_start(1, 4, 5, 6, 7)
+    run_of_four(0, 2, 3)
     backward(1)
     gb[...] = (hb[...] * mix[...]).astype(BF16)
     ub[...] = (hb[...] * act[...]).astype(BF16)
+    ring_step(0, 0)
     row_grads(0)
     send(4)
-    run_of_four(0, 4)
-    run_of_four(0, 5)
-    run_of_four(1, 0)
-    run_of_four(1, 1)
+    run_of_four(1, 0, 1)
     ring_step(0, 1)
-    run_of_four(1, 2)
-    run_of_four(1, 3)
+    run_of_four(0, 4, 5)
+    ring_step(1, 0)
     row_grads(1)
     send(5)
-    ring_step(1, 0)
-    run_of_four(0, 6)
-    run_of_four(0, 7)
+    run_of_four(1, 2, 3)
     ring_step(0, 2)
-    run_of_four(1, 4)
-    run_of_four(1, 5)
+    run_of_four(0, 6, 7)
     ring_step(1, 1)
+    run_of_four(1, 4, 5)
     ring_step(0, 3)
-    run_of_four(1, 6)
-    run_of_four(1, 7)
+    run_of_four(1, 6, 7)
     ring_step(1, 2)
     arrive(4)
     combine(0)
+    ring_end(0)
     ring_step(1, 3)
-    ring_end(0)
     arrive(5)
     combine(1)
     ring_end(1)

time: 97.5 us -> 92.6 us (0.950)
  the two profiles are of different devices: /device:TPU:78 before, /device:TPU:8 now
where the time goes in v4:
time: 92.6 us; the launch traced here: 92.4 us
  Pallas kernels  90.3 us (98%)
  local copies, waits for them, and re-layouts  1.42 us (2%)
    pallas_call x1, Pallas kernels, body(): pl.pallas_call(functools.partial(kernel, nz, experts // 4), out_shape=(pl...  90.3 us

profile of v4, /device:TPU:8, one launch (start us, length us, event | category | flops | bytes accessed | tf_op | source)
XLA Modules:
  0.0 92.4 jit_solution(9128969246931998286)
XLA Ops:
  0.6 90.3 %shard_map.86 = (bf16[128,2048]{1,0:T(8,128)(2,1)S(1)}, f32[8,2048]{1,0:T(8,128)S(1)}) custom-call(bf16[128,2048]{1,0:T(8,128)(2,1)} %tok_hbm.1, bf16[128,2048]{1,0:T(8,128)(2,1)} %cot_hbm.1, s32[2,128]{1,0:T(2,128)} %bitcast.10, bf16[2,128]{1,0:T(2,128)(2,1)} %bitcast.11, bf16[2048,512]{1,0:T(8,128)(2,1)} %bitcast.7, bf16[2048,512]{1,0:T(8,128)(2,1)} %bitcast.8, ...), custom_call_target="tpu_custom_call" | custom-call | flops 3623878656 | bytes 8388608 | tf_op jit(solution)/shard_map/pallas_call | solution.py:394
  90.9 0.8 copy.11
  91.7 0.6 copy.12

commit v5 on v4

--- a/solution.py
+++ b/solution.py
@@ -251,7 +251,7 @@
             part[h, :, lo] = nn(hidt[...], sr[h, 0:rows, lo])
             return carry
 
-        lax.fori_loop(0, half // 256, tile, 0)
+        lax.fori_loop(0, half // 256, tile, 0, unroll=True)
 
     def y_start(h, *js):
         for j in js:
@@ -298,7 +298,7 @@
             hb[:, f] = v if h == 0 else hb[:, f] + v
             return carry
 
-        lax.fori_loop(0, hidden // tile_f, back, 0)
+        lax.fori_loop(0, hidden // tile_f, back, 0, unroll=True)
 
     def row_grads(h):
         def tile(t, carry):
@@ -307,7 +307,7 @@
             rd[h, 0:rows, pl.ds(lo, 256)] = (nt(gb[...], wg[w, :]) + nt(ub[...], wu[w, :])).astype(BF16)
             return carry
 
-        lax.fori_loop(0, half // 256, tile, 0)
+        lax.fori_loop(0, half // 256, tile, 0, unroll=True)
         pack(rd, h)
 
     def combine(h):
@@ -330,36 +330,36 @@
     arrive(3)
     unpack(sr, 1)
     products(1)
-    y_start(1, 0, 1)
+    y_start(1, 0, 1, 2, 3)
     y_start(0, 4, 5)
-    y_start(1, 2, 3)
+    y_start(1, 4, 5)
     y_start(0, 6, 7)
-    y_start(1, 4, 5, 6, 7)
+    y_start(1, 6, 7)
     run_of_four(0, 2, 3)
     backward(1)
     gb[...] = (hb[...] * mix[...]).astype(BF16)
     ub[...] = (hb[...] * act[...]).astype(BF16)
     ring_step(0, 0)
+    run_of_four(1, 0, 1)
     row_grads(0)
     send(4)
-    run_of_four(1, 0, 1)
+    run_of_four(1, 2, 3)
     ring_step(0, 1)
-    run_of_four(0, 4, 5)
     ring_step(1, 0)
     row_grads(1)
     send(5)
-    run_of_four(1, 2, 3)
+    run_of_four(0, 4, 5)
+    run_of_four(1, 4, 5)
+    ring_step(1, 1)
     ring_step(0, 2)
     run_of_four(0, 6, 7)
-    ring_step(1, 1)
-    run_of_four(1, 4, 5)
-    ring_step(0, 3)
     run_of_four(1, 6, 7)
     ring_step(1, 2)
+    ring_step(0, 3)
     arrive(4)
     combine(0)
+    ring_step(1, 3)
     ring_end(0)
-    ring_step(1, 3)
     arrive(5)
     combine(1)
     ring_end(1)

time: 92.6 us -> 92.9 us (level)
  the two profiles are of different devices: /device:TPU:8 before, /device:TPU:14 now
where the time goes in v5:
time: 92.9 us; the launch traced here: 92.7 us
  Pallas kernels  90.6 us (98%)
  local copies, waits for them, and re-layouts  1.42 us (2%)
    pallas_call x1, Pallas kernels, body(): pl.pallas_call(functools.partial(kernel, nz, experts // 4), out_shape=(pl...  90.6 us

profile of v5, /device:TPU:14, one launch (start us, length us, event | category | flops | bytes accessed | tf_op | source)
XLA Modules:
  0.0 92.7 jit_solution(15264644318742476152)
XLA Ops:
  0.6 90.6 %shard_map.86 = (bf16[128,2048]{1,0:T(8,128)(2,1)S(1)}, f32[8,2048]{1,0:T(8,128)S(1)}) custom-call(bf16[128,2048]{1,0:T(8,128)(2,1)} %tok_hbm.1, bf16[128,2048]{1,0:T(8,128)(2,1)} %cot_hbm.1, s32[2,128]{1,0:T(2,128)} %bitcast.10, bf16[2,128]{1,0:T(2,128)(2,1)} %bitcast.11, bf16[2048,512]{1,0:T(8,128)(2,1)} %bitcast.7, bf16[2048,512]{1,0:T(8,128)(2,1)} %bitcast.8, ...), custom_call_target="tpu_custom_call" | custom-call | flops 3623878656 | bytes 8388608 | tf_op jit(solution)/shard_map/pallas_call | solution.py:394
  91.3 0.8 copy.11
  92.1 0.6 copy.12
